TPU v7x, 32 devices: a whole 2x2x4 slice. The times are simulated.
32 devices in a mesh: blk: 8 (over z, core), tiles: 4 (over y, x).
Axes of the slice: x: 2, y: 2, z: 4, core: 2. Of those that a mesh axis runs over, the one named last changes fastest.
Arguments:
- tiles: bfloat16 [32, 128, 128, 128], P(('blk', 'tiles')), may hold values from -6 to 6
- live: int32 [32], P(('blk', 'tiles')), may hold values 0 or 1
- templates: bfloat16 [8, 64, 4096], P('blk', None, 'tiles'), may hold values from -0.01171875 to 0.01171875
Outputs:
- peak: float32 [32, 2, 128, 128], P(('blk', 'tiles'))
- mean_score: float32 [32, 2, 128, 128], P(('blk', 'tiles'))
All inputs are finite; a program needn't handle non-finite values. No bound on the sum of `live` on one device may be relied on, other than what follows from the above.
Results may differ from a plain program's by a relative error of at most 0.0093.
Values may be sent and summed in bfloat16 or wider, within the bound.
A program may use at most 64 MiB of HBM per device.

v0:
```python
import math

import jax
import jax.numpy as jnp
from jax import lax
from jax.sharding import PartitionSpec as P

OUTZ = 2


def tables(count, width):
    rows = jnp.arange(count, dtype=jnp.int32)[:, None]
    cols = jnp.arange(width, dtype=jnp.int32)[None, :]
    phase = (rows * cols % count).astype(jnp.float32) * (2.0 * math.pi / count)
    return (jnp.cos(phase).astype(jnp.bfloat16), jnp.sin(phase).astype(jnp.bfloat16))


def mult(form, left, right):
    return jnp.einsum(form, left, right, preferred_element_type=jnp.float32)


def spectrum(volume, cosine_y, sine_y, cosine_x, sine_x):
    first_real = mult("...vu,kv->...ku", volume, cosine_y).astype(jnp.bfloat16)
    first_imag = (-mult("...vu,kv->...ku", volume, sine_y)).astype(jnp.bfloat16)
    out_real = (
        mult("...ku,hu->...kh", first_real, cosine_x) + mult("...ku,hu->...kh", first_imag, sine_x)
    ).astype(jnp.bfloat16)
    out_imag = (
        mult("...ku,hu->...kh", first_imag, cosine_x) - mult("...ku,hu->...kh", first_real, sine_x)
    ).astype(jnp.bfloat16)
    return (out_real, out_imag)


def correlate(
    pattern_real, pattern_imag, spectra_real, spectra_imag, cosine_x, sine_x, cosine_y, sine_y
):
    edge = pattern_real.shape[0]
    plane_real = []
    plane_imag = []
    for offset in range(OUTZ):
        moved_real = jnp.roll(spectra_real, -offset, axis=-3)[..., :edge, :, :]
        moved_imag = jnp.roll(spectra_imag, -offset, axis=-3)[..., :edge, :, :]
        sum_real = mult("wkh,...wkh->...kh", pattern_real, moved_real) + mult(
            "wkh,...wkh->...kh", pattern_imag, moved_imag
        )
        sum_imag = mult("wkh,...wkh->...kh", pattern_real, moved_imag) - mult(
            "wkh,...wkh->...kh", pattern_imag, moved_real
        )
        plane_real.append(sum_real.astype(jnp.bfloat16))
        plane_imag.append(sum_imag.astype(jnp.bfloat16))
    prod_real = jnp.stack(plane_real, axis=-3)
    prod_imag = jnp.stack(plane_imag, axis=-3)
    back_real = (
        mult("...dkh,hx->...dkx", prod_real, cosine_x)
        - mult("...dkh,hx->...dkx", prod_imag, sine_x)
    ).astype(jnp.bfloat16)
    back_imag = (
        mult("...dkh,hx->...dkx", prod_real, sine_x)
        + mult("...dkh,hx->...dkx", prod_imag, cosine_x)
    ).astype(jnp.bfloat16)
    scale = 1.0 / (cosine_x.shape[0] * cosine_y.shape[0])
    return (
        mult("...dkx,ky->...dyx", back_real, cosine_y)
        - mult("...dkx,ky->...dyx", back_imag, sine_y)
    ) * scale


def shards(tiles, live, templates):
    slots, depth, height, width = tiles.shape
    edge = templates.shape[1]
    cosine_x, sine_x = tables(width, width)
    cosine_y, sine_y = tables(height, height)
    count = templates.shape[0] * lax.axis_size("blk")
    flags = live > 0
    spectra_real, spectra_imag = spectrum(tiles, cosine_y, sine_y, cosine_x, sine_x)

    def scorer(pattern_real, pattern_imag):
        return correlate(
            pattern_real,
            pattern_imag,
            spectra_real,
            spectra_imag,
            cosine_x,
            sine_x,
            cosine_y,
            sine_y,
        )

    def update(carry, template):
        volume = template.reshape(edge, edge, edge)
        pattern_real, pattern_imag = spectrum(
            volume, cosine_y[:, :edge], sine_y[:, :edge], cosine_x[:, :edge], sine_x[:, :edge]
        )
        scores = scorer(pattern_real, pattern_imag)
        return (jnp.maximum(carry[0], scores), carry[1] + scores)

    initial = (
        jnp.full((slots, OUTZ, height, width), -jnp.inf, jnp.float32),
        jnp.zeros((slots, OUTZ, height, width), jnp.float32),
    )
    whole = lax.all_gather(templates, "tiles", axis=2, tiled=True)
    piece = lax.all_gather(whole, "blk", axis=0, tiled=True)

    def inner(index, state):
        return update(state, piece[index])

    highest, total = lax.fori_loop(0, piece.shape[0], inner, initial)
    factor = flags.astype(jnp.float32)[:, None, None, None]
    return (highest * factor, total / count * factor)


def solution(mesh):
    placed = (P(("blk", "tiles"), None, None, None), P(("blk", "tiles")), P("blk", None, "tiles"))
    return jax.shard_map(
        shards,
        mesh=mesh,
        in_specs=placed,
        out_specs=(P(("blk", "tiles"), None, None, None), P(("blk", "tiles"), None, None, None)),
        check_vma=False,
    )
```

profile of v0, /device:TPU:0, one launch (start us, length us, event | category | flops | bytes accessed | tf_op | source)
XLA Modules:
  0.0 179.8 jit_solution(9747681309156040541)
XLA Ops:
  7.2 13.2 %all_gather.6 = bf16[1,64,4096]{2,1,0:T(8,128)(2,1)} all-gather(bf16[1,64,1024]{2,1,0:T(8,128)(2,1)} %param.7), channel_id=1, replica_groups=mesh['blk'=8,'tiles'=4] {'tiles'}, dimensions={2}, use_global_device_ids=true | all-gather | bytes 655360 | tf_op jit(solution)/shard_map/all_gather | solution.py:101
  21.4 3.9 %fusion.60 = bf16[128,128,128]{2,0,1:T(8,128)(2,1)S(1)} fusion(bf16[1,128,128,128]{3,2,1,0:T(8,128)(2,1)} %param.5), kind=kOutput, calls=%fused_computation.83 | convolution fusion | flops 539213824 | bytes 8388608 | tf_op jit(solution)/shard_map/...vu,kv->...ku/dot_general | solution.py:19
  25.2 1.5 fusion.49
  26.8 1.5 fusion.54
  28.2 1.5 fusion.52
  29.7 3.5 %fusion.50 = bf16[1,128,128,128]{3,2,1,0:T(8,128)(2,1)} fusion(f32[128,128,128]{2,1,0:T(8,128)S(1)} %fusion.54, bf16[128,128,128]{2,1,0:T(8,128)(2,1)S(1)} %fusion.49), kind=kOutput, calls=%fused_computation.73 | convolution fusion | flops 541310976 | bytes 16777216 | tf_op jit(solution)/shard_map/...ku,hu->...kh/dot_general | solution.py:19
  33.2 3.5 %fusion.51 = bf16[1,128,128,128]{3,2,1,0:T(8,128)(2,1)} fusion(f32[128,128,128]{2,1,0:T(8,128)S(1)} %fusion.52, bf16[128,128,128]{2,1,0:T(8,128)(2,1)S(1)} %fusion.49), kind=kOutput, calls=%fused_computation.74 | convolution fusion | flops 541310976 | bytes 16777216 | tf_op jit(solution)/shard_map/...ku,hu->...kh/dot_general | solution.py:19
  36.6 31.5 %all-gather.2.cloned.1.call-done = bf16[8,64,4096]{2,1,0:T(8,128)(2,1)} async-done(((bf16[1,64,4096]{2,1,0:T(8,128)(2,1)}), bf16[8,64,4096]{2,1,0:T(8,128)(2,1)}) %all-gather.2.cloned.1.call-update) | async-done | bytes 4194320 | tf_op jit(solution)/shard_map/all_gather | solution.py:102
  68.1 103.3 %while.18 = (s32[]{:T(128)}, f32[1,2,128,128]{2,3,1,0:T(8,128)S(1)}, f32[1,2,128,128]{2,3,1,0:T(8,128)S(1)}, bf16[8,64,4096]{2,1,0:T(8,128)(2,1)}, bf16[128,128]...) while((s32[]{:T(128)}, ...), condition=%wide.region_1.2_spmd.clone.clone, body=%wide.region_0.1_spmd.clone.clone.sunk | while | flops 750714880 | bytes 76447912 | solution.py:107
  68.1 1.1 constant_dynamic-slice_fusion.2
  69.2 1.1 squeeze.11
  70.8 0.8 fusion.154
  72.1 0.8 subtract_convert_fusion.5
  72.8 0.8 fusion.156
  74.2 1.5 copy-done.1
  75.7 4.1 %fusion.157 = (f32[128,128]{1,0:T(8,128)S(1)}, f32[128,128]{1,0:T(8,128)S(1)}, f32[128,128]{1,0:T(8,128)S(1)}, f32[128,128]{1,0:T(8,128)S(1)}, f32[128,128]{1,0:...) fusion(bf16[1,128,128,128]{3,2,1,0:T(8,128)(2,1)S(1)} %copy-done.2, ...), kind=kOutput, calls=%fused_computation.10.clone.1 | convolution fusion | flops 159252480 | bytes 16269312 | tf_op jit(solution)/shard_map/while/body/eval_jaxpr/...ku,hu->...kh/dot_general | solution.py:19
  81.0 1.1 constant_dynamic-slice_fusion.2
  82.1 1.1 squeeze.11
  83.7 0.8 fusion.154
  85.0 0.8 subtract_convert_fusion.5
  85.8 0.8 fusion.156
  87.1 1.5 copy-done.1
  88.6 4.1 %fusion.157 = (f32[128,128]{1,0:T(8,128)S(1)}, f32[128,128]{1,0:T(8,128)S(1)}, f32[128,128]{1,0:T(8,128)S(1)}, f32[128,128]{1,0:T(8,128)S(1)}, f32[128,128]{1,0:...) fusion(bf16[1,128,128,128]{3,2,1,0:T(8,128)(2,1)S(1)} %copy-done.2, ...), kind=kOutput, calls=%fused_computation.10.clone.1 | convolution fusion | flops 159252480 | bytes 16269312 | tf_op jit(solution)/shard_map/while/body/eval_jaxpr/...ku,hu->...kh/dot_general | solution.py:19
  93.9 1.1 constant_dynamic-slice_fusion.2
  95.0 1.1 squeeze.11
  96.6 0.8 fusion.154
  97.9 0.8 subtract_convert_fusion.5
  98.7 0.8 fusion.156
  100.1 1.5 copy-done.1
  101.5 4.1 %fusion.157 = (f32[128,128]{1,0:T(8,128)S(1)}, f32[128,128]{1,0:T(8,128)S(1)}, f32[128,128]{1,0:T(8,128)S(1)}, f32[128,128]{1,0:T(8,128)S(1)}, f32[128,128]{1,0:...) fusion(bf16[1,128,128,128]{3,2,1,0:T(8,128)(2,1)S(1)} %copy-done.2, ...), kind=kOutput, calls=%fused_computation.10.clone.1 | convolution fusion | flops 159252480 | bytes 16269312 | tf_op jit(solution)/shard_map/while/body/eval_jaxpr/...ku,hu->...kh/dot_general | solution.py:19
  106.9 1.1 constant_dynamic-slice_fusion.2
  107.9 1.1 squeeze.11
  109.5 0.8 fusion.154
  110.8 0.8 subtract_convert_fusion.5
  111.6 0.8 fusion.156
  113.0 1.5 copy-done.1
  114.5 4.1 %fusion.157 = (f32[128,128]{1,0:T(8,128)S(1)}, f32[128,128]{1,0:T(8,128)S(1)}, f32[128,128]{1,0:T(8,128)S(1)}, f32[128,128]{1,0:T(8,128)S(1)}, f32[128,128]{1,0:...) fusion(bf16[1,128,128,128]{3,2,1,0:T(8,128)(2,1)S(1)} %copy-done.2, ...), kind=kOutput, calls=%fused_computation.10.clone.1 | convolution fusion | flops 159252480 | bytes 16269312 | tf_op jit(solution)/shard_map/while/body/eval_jaxpr/...ku,hu->...kh/dot_general | solution.py:19
  119.8 1.1 constant_dynamic-slice_fusion.2
  120.9 1.1 squeeze.11
  122.5 0.8 fusion.154
  123.7 0.8 subtract_convert_fusion.5
  124.5 0.8 fusion.156
  125.9 1.5 copy-done.1
  127.4 4.1 %fusion.157 = (f32[128,128]{1,0:T(8,128)S(1)}, f32[128,128]{1,0:T(8,128)S(1)}, f32[128,128]{1,0:T(8,128)S(1)}, f32[128,128]{1,0:T(8,128)S(1)}, f32[128,128]{1,0:...) fusion(bf16[1,128,128,128]{3,2,1,0:T(8,128)(2,1)S(1)} %copy-done.2, ...), kind=kOutput, calls=%fused_computation.10.clone.1 | convolution fusion | flops 159252480 | bytes 16269312 | tf_op jit(solution)/shard_map/while/body/eval_jaxpr/...ku,hu->...kh/dot_general | solution.py:19
  132.7 1.1 constant_dynamic-slice_fusion.2
  133.8 1.1 squeeze.11
  136.6 0.8 subtract_convert_fusion.5
  137.4 0.8 fusion.156
  138.8 1.5 copy-done.1
  140.3 4.1 %fusion.157 = (f32[128,128]{1,0:T(8,128)S(1)}, f32[128,128]{1,0:T(8,128)S(1)}, f32[128,128]{1,0:T(8,128)S(1)}, f32[128,128]{1,0:T(8,128)S(1)}, f32[128,128]{1,0:...) fusion(bf16[1,128,128,128]{3,2,1,0:T(8,128)(2,1)S(1)} %copy-done.2, ...), kind=kOutput, calls=%fused_computation.10.clone.1 | convolution fusion | flops 159252480 | bytes 16269312 | tf_op jit(solution)/shard_map/while/body/eval_jaxpr/...ku,hu->...kh/dot_general | solution.py:19
  145.6 1.1 constant_dynamic-slice_fusion.2
  146.7 1.1 squeeze.11
  148.3 0.8 fusion.154
  149.6 0.8 subtract_convert_fusion.5
  150.3 0.8 fusion.156
  151.7 1.5 copy-done.1
  153.2 4.1 %fusion.157 = (f32[128,128]{1,0:T(8,128)S(1)}, f32[128,128]{1,0:T(8,128)S(1)}, f32[128,128]{1,0:T(8,128)S(1)}, f32[128,128]{1,0:T(8,128)S(1)}, f32[128,128]{1,0:...) fusion(bf16[1,128,128,128]{3,2,1,0:T(8,128)(2,1)S(1)} %copy-done.2, ...), kind=kOutput, calls=%fused_computation.10.clone.1 | convolution fusion | flops 159252480 | bytes 16269312 | tf_op jit(solution)/shard_map/while/body/eval_jaxpr/...ku,hu->...kh/dot_general | solution.py:19
  158.5 1.1 constant_dynamic-slice_fusion.2
  159.6 1.1 squeeze.11
  161.2 0.8 fusion.154
  162.5 0.8 subtract_convert_fusion.5
  163.3 0.8 fusion.156
  164.7 1.5 copy-done.1
  166.1 4.1 %fusion.157 = (f32[128,128]{1,0:T(8,128)S(1)}, f32[128,128]{1,0:T(8,128)S(1)}, f32[128,128]{1,0:T(8,128)S(1)}, f32[128,128]{1,0:T(8,128)S(1)}, f32[128,128]{1,0:...) fusion(bf16[1,128,128,128]{3,2,1,0:T(8,128)(2,1)S(1)} %copy-done.2, ...), kind=kOutput, calls=%fused_computation.10.clone.1 | convolution fusion | flops 159252480 | bytes 16269312 | tf_op jit(solution)/shard_map/while/body/eval_jaxpr/...ku,hu->...kh/dot_general | solution.py:19
  (100 shorter events, 24.0 us)
Async XLA Ops:
  7.2 60.9 %all-gather.2.cloned.1.call-start = ((), (), s32[]{:S(2)}) async-start(), calls=%async_computation | async-start | bytes 4718592 | tf_op jit(solution)/shard_map/all_gather | solution.py:102
  21.3 3.9 %copy-start = (bf16[1,128,128,128]{3,2,1,0:T(8,128)(2,1)S(1)}, bf16[1,128,128,128]{3,2,1,0:T(8,128)(2,1)}, u32[]{:S(2)}) copy-start(bf16[1,128,128,128]{3,2,1,0:T(8,128)(2,1)} %param.5) | copy-start | bytes 12582916
  72.0 2.2 %copy-start.2 = (bf16[1,128,128,128]{3,2,1,0:T(8,128)(2,1)S(1)}, bf16[1,128,128,128]{3,2,1,0:T(8,128)(2,1)}, u32[]{:S(2)}) copy-start(bf16[1,128,128,128]{3,2,1,0:T(8,128)(2,1)} %get-tuple-element.405) | copy-start | bytes 12582916 | tf_op jit(solution)/shard_map/while
  72.8 2.9 %copy-start.1 = (bf16[1,128,128,128]{3,2,1,0:T(8,128)(2,1)S(1)}, bf16[1,128,128,128]{3,2,1,0:T(8,128)(2,1)}, u32[]{:S(2)}) copy-start(bf16[1,128,128,128]{3,2,1,0:T(8,128)(2,1)} %get-tuple-element.404) | copy-start | bytes 12582916 | tf_op jit(solution)/shard_map/while
  85.0 2.2 %copy-start.2 = (bf16[1,128,128,128]{3,2,1,0:T(8,128)(2,1)S(1)}, bf16[1,128,128,128]{3,2,1,0:T(8,128)(2,1)}, u32[]{:S(2)}) copy-start(bf16[1,128,128,128]{3,2,1,0:T(8,128)(2,1)} %get-tuple-element.405) | copy-start | bytes 12582916 | tf_op jit(solution)/shard_map/while
  85.7 2.9 %copy-start.1 = (bf16[1,128,128,128]{3,2,1,0:T(8,128)(2,1)S(1)}, bf16[1,128,128,128]{3,2,1,0:T(8,128)(2,1)}, u32[]{:S(2)}) copy-start(bf16[1,128,128,128]{3,2,1,0:T(8,128)(2,1)} %get-tuple-element.404) | copy-start | bytes 12582916 | tf_op jit(solution)/shard_map/while
  97.9 2.2 %copy-start.2 = (bf16[1,128,128,128]{3,2,1,0:T(8,128)(2,1)S(1)}, bf16[1,128,128,128]{3,2,1,0:T(8,128)(2,1)}, u32[]{:S(2)}) copy-start(bf16[1,128,128,128]{3,2,1,0:T(8,128)(2,1)} %get-tuple-element.405) | copy-start | bytes 12582916 | tf_op jit(solution)/shard_map/while
  98.7 2.9 %copy-start.1 = (bf16[1,128,128,128]{3,2,1,0:T(8,128)(2,1)S(1)}, bf16[1,128,128,128]{3,2,1,0:T(8,128)(2,1)}, u32[]{:S(2)}) copy-start(bf16[1,128,128,128]{3,2,1,0:T(8,128)(2,1)} %get-tuple-element.404) | copy-start | bytes 12582916 | tf_op jit(solution)/shard_map/while
  110.8 2.2 %copy-start.2 = (bf16[1,128,128,128]{3,2,1,0:T(8,128)(2,1)S(1)}, bf16[1,128,128,128]{3,2,1,0:T(8,128)(2,1)}, u32[]{:S(2)}) copy-start(bf16[1,128,128,128]{3,2,1,0:T(8,128)(2,1)} %get-tuple-element.405) | copy-start | bytes 12582916 | tf_op jit(solution)/shard_map/while
  111.6 2.9 %copy-start.1 = (bf16[1,128,128,128]{3,2,1,0:T(8,128)(2,1)S(1)}, bf16[1,128,128,128]{3,2,1,0:T(8,128)(2,1)}, u32[]{:S(2)}) copy-start(bf16[1,128,128,128]{3,2,1,0:T(8,128)(2,1)} %get-tuple-element.404) | copy-start | bytes 12582916 | tf_op jit(solution)/shard_map/while
  123.7 2.2 %copy-start.2 = (bf16[1,128,128,128]{3,2,1,0:T(8,128)(2,1)S(1)}, bf16[1,128,128,128]{3,2,1,0:T(8,128)(2,1)}, u32[]{:S(2)}) copy-start(bf16[1,128,128,128]{3,2,1,0:T(8,128)(2,1)} %get-tuple-element.405) | copy-start | bytes 12582916 | tf_op jit(solution)/shard_map/while
  124.5 2.9 %copy-start.1 = (bf16[1,128,128,128]{3,2,1,0:T(8,128)(2,1)S(1)}, bf16[1,128,128,128]{3,2,1,0:T(8,128)(2,1)}, u32[]{:S(2)}) copy-start(bf16[1,128,128,128]{3,2,1,0:T(8,128)(2,1)} %get-tuple-element.404) | copy-start | bytes 12582916 | tf_op jit(solution)/shard_map/while
  136.6 2.2 %copy-start.2 = (bf16[1,128,128,128]{3,2,1,0:T(8,128)(2,1)S(1)}, bf16[1,128,128,128]{3,2,1,0:T(8,128)(2,1)}, u32[]{:S(2)}) copy-start(bf16[1,128,128,128]{3,2,1,0:T(8,128)(2,1)} %get-tuple-element.405) | copy-start | bytes 12582916 | tf_op jit(solution)/shard_map/while
  137.4 2.9 %copy-start.1 = (bf16[1,128,128,128]{3,2,1,0:T(8,128)(2,1)S(1)}, bf16[1,128,128,128]{3,2,1,0:T(8,128)(2,1)}, u32[]{:S(2)}) copy-start(bf16[1,128,128,128]{3,2,1,0:T(8,128)(2,1)} %get-tuple-element.404) | copy-start | bytes 12582916 | tf_op jit(solution)/shard_map/while
  149.5 2.2 %copy-start.2 = (bf16[1,128,128,128]{3,2,1,0:T(8,128)(2,1)S(1)}, bf16[1,128,128,128]{3,2,1,0:T(8,128)(2,1)}, u32[]{:S(2)}) copy-start(bf16[1,128,128,128]{3,2,1,0:T(8,128)(2,1)} %get-tuple-element.405) | copy-start | bytes 12582916 | tf_op jit(solution)/shard_map/while
  150.3 2.9 %copy-start.1 = (bf16[1,128,128,128]{3,2,1,0:T(8,128)(2,1)S(1)}, bf16[1,128,128,128]{3,2,1,0:T(8,128)(2,1)}, u32[]{:S(2)}) copy-start(bf16[1,128,128,128]{3,2,1,0:T(8,128)(2,1)} %get-tuple-element.404) | copy-start | bytes 12582916 | tf_op jit(solution)/shard_map/while
  162.5 2.2 %copy-start.2 = (bf16[1,128,128,128]{3,2,1,0:T(8,128)(2,1)S(1)}, bf16[1,128,128,128]{3,2,1,0:T(8,128)(2,1)}, u32[]{:S(2)}) copy-start(bf16[1,128,128,128]{3,2,1,0:T(8,128)(2,1)} %get-tuple-element.405) | copy-start | bytes 12582916 | tf_op jit(solution)/shard_map/while
  163.3 2.9 %copy-start.1 = (bf16[1,128,128,128]{3,2,1,0:T(8,128)(2,1)S(1)}, bf16[1,128,128,128]{3,2,1,0:T(8,128)(2,1)}, u32[]{:S(2)}) copy-start(bf16[1,128,128,128]{3,2,1,0:T(8,128)(2,1)} %get-tuple-element.404) | copy-start | bytes 12582916 | tf_op jit(solution)/shard_map/while
Sparse Core Ops, SparseCore 0:
  20.5 47.5 all-gather.1
where the time goes:
time: 181 us; the launch traced here: 180 us
  matrix products  82.8 us (46%)
  local copies, waits for them, and re-layouts  34.6 us (19%)
  waiting for transfers between devices  31.5 us (17%)
  between operations  14.8 us (8%)
  blocking collectives  13.2 us (7%)
  other arithmetic  1.95 us (1%)
    dot_general x86, matrix products, mult(): return jnp.einsum(form, left, right, preferred_element_type=jnp.float32)  82.8 us
    all_gather x1, waiting for transfers between devices, shards(): piece = lax.all_gather(whole, 'blk', axis=0, tiled=True)  31.5 us
    while x32, local copies, waits for them, and re-layouts  16.8 us
    all_gather x1, blocking collectives, shards(): whole = lax.all_gather(templates, 'tiles', axis=2, tiled=True)  13.2 us
    squeeze x8, local copies, waits for them, and re-layouts, update(): volume = template.reshape(edge, edge, edge)  9 us
    dynamic_slice x8, local copies, waits for them, and re-layouts, inner(): return update(state, piece[index])  8.64 us
  transfers between devices with their start and end apart: 1, of which 1 were waited for; matrix products, arithmetic and copies ran while one was open for 9% of the time, Pallas kernels for 0%

commit v1 on v0

v1 whole, which is shorter than its diff:
```python
import functools
import math

import jax
import jax.numpy as jnp
import numpy as np
from jax import lax
from jax.experimental import pallas as pl
from jax.experimental.pallas import tpu as pltpu
from jax.sharding import PartitionSpec as P

OUTZ = 2
MESH = pl.DeviceIdType.MESH
BF = jnp.bfloat16
F32 = jnp.float32


def tables(count, width):
    phase = (np.arange(count)[:, None] * np.arange(width)[None, :] % count).astype(np.float32)
    phase = phase * np.float32(2.0 * math.pi / count)
    return np.cos(phase).astype(np.float32), np.sin(phase).astype(np.float32)


def constants(height, width, edge, padded):
    half = height // 2 + 1
    cy, sy = tables(height, height)
    cx, sx = tables(width, width)
    rows = np.zeros((2 * padded, height), np.float32)
    rows[:half] = cy[:half]
    rows[padded : padded + half] = -sy[:half]
    tile_x = np.block([[cx.T, -sx.T], [sx.T, cx.T]])
    ce, se = cx[:, :edge].T, sx[:, :edge].T
    zero = np.zeros_like(ce)
    pair_x = np.block(
        [[ce, -se, zero, zero], [zero, zero, ce, -se], [se, ce, zero, zero], [zero, zero, se, ce]]
    )
    back_x = np.block([[cx, sx], [-sx, cx]])
    weight = np.full((half,), 2.0, np.float32)
    weight[0] = 1.0
    if height % 2 == 0:
        weight[-1] = 1.0
    weight = weight / (height * width)
    back_y = np.zeros((height, 2 * padded), np.float32)
    back_y[:, :half] = cy[:, :half].astype(jnp.bfloat16).astype(np.float32) * weight
    back_y[:, padded : padded + half] = -sy[:, :half].astype(jnp.bfloat16).astype(np.float32) * weight
    parts = (rows, rows[:, :edge], tile_x, pair_x, back_x, back_y)
    return tuple(jnp.asarray(np.ascontiguousarray(p).astype(jnp.bfloat16)) for p in parts)


def dot(left, right):
    return jnp.dot(left, right, preferred_element_type=F32)


def kernel(
    cfg, tile_hbm, own, tile_y, pat_y, tile_x, pair_x, back_x, back_y, peak, total,
    tile_buf, pieces, spectra, pattern, acc, tile_sem, send_sem, recv_sem,
):
    chips, count_t, padded, groups, edge, width = cfg
    bits = count_t.bit_length() - 1
    planes = tile_buf.shape[0]
    blk = lax.axis_index("blk")
    t = lax.axis_index("tiles")
    chip, core = blk // 2, blk % 2
    fetch = pltpu.make_async_copy(tile_hbm.at[0, pl.ds(0, planes)], tile_buf, tile_sem)
    fetch.start()

    def other(bit):
        size = 1 << bit
        return (blk, t + size - 2 * size * ((t // size) % 2))

    buddy = (blk + 1 - 2 * core, t)
    line = [(((chip + k) % chips) * 2 + core, t) for k in range(1, chips)]
    peers = line + [other(b) for b in range(bits)] + [buddy]
    barrier = pltpu.get_barrier_semaphore()
    for peer in peers:
        pl.semaphore_signal(barrier, inc=1, device_id=peer, device_id_type=MESH)
    pieces[0, 0, 0] = own[...]
    pl.semaphore_wait(barrier, len(peers))

    sends = []

    def send(src, dst, device):
        copy = pltpu.make_async_remote_copy(
            src_ref=pieces.at[src],
            dst_ref=pieces.at[dst],
            send_sem=send_sem.at[len(sends)],
            recv_sem=recv_sem.at[dst],
            device_id=device,
            device_id_type=MESH,
        )
        copy.start()
        sends.append(copy)

    def arrive(slot):
        pltpu.make_async_copy(pieces.at[slot], pieces.at[slot], recv_sem.at[slot]).wait()

    def service(k, stage):
        order = [(b + k) % bits for b in range(bits)]
        have = [0]
        for b in order[: max(stage - 1, 0)]:
            have = have + [h ^ (1 << b) for h in have]
        fresh = have
        if stage > 0:
            fresh = [h ^ (1 << order[stage - 1]) for h in have]
            have = have + fresh
        if stage > 0 or k > 0:
            for h in fresh:
                arrive((k, 0, h))
        if stage < bits:
            step = 1 << order[stage]
            for h in have:
                send((k, 0, h), (k, 0, h ^ step), other(order[stage]))
        for h in fresh:
            send((k, 0, h), (k, 1, h), buddy)

    for k in range(1, chips):
        send((0, 0, 0), (k, 0, 0), line[k - 1])
    service(0, 0)

    def tile_pairs(low, high):
        def body(p, carry):
            both = jnp.concatenate([tile_buf[2 * p], tile_buf[2 * p + 1]], axis=1)
            first = dot(tile_y[...], both).astype(BF)
            left = jnp.concatenate(
                [
                    jnp.concatenate(
                        [
                            first[:padded, j * width : (j + 1) * width],
                            first[padded:, j * width : (j + 1) * width],
                        ],
                        axis=1,
                    )
                    for j in range(2)
                ],
                axis=0,
            )
            out = dot(left, tile_x[...])
            spectra[2 * p] = out[:padded]
            spectra[2 * p + 1] = out[padded:]
            return carry

        lax.fori_loop(low, high, body, 0)

    def rotation(k, side, begin):
        acc[...] = jnp.zeros_like(acc)
        depth = 8
        lanes = depth * edge

        def body(q, carry):
            columns = pl.ds(pl.multiple_of(q * lanes, lanes), lanes)
            parts = []
            for source in range(count_t):
                slot = 0
                for b in range(bits):
                    size = 1 << b
                    slot = slot + size * (((source // size) + (t // size)) % 2)
                parts.append(pieces[k, side, slot, :, columns])
            first = dot(pat_y[...], jnp.concatenate(parts, axis=0)).astype(BF)
            left = jnp.concatenate(
                [
                    jnp.concatenate(
                        [
                            first[:padded, j * 2 * edge : (j + 1) * 2 * edge],
                            first[padded:, j * 2 * edge : (j + 1) * 2 * edge],
                        ],
                        axis=1,
                    )
                    for j in range(depth // 2)
                ],
                axis=0,
            )
            pattern[...] = dot(left, pair_x[...])
            for g in range(groups):
                rows = slice(8 * g, 8 * g + 8)
                sums = [acc[i, rows, :] for i in range(2 * OUTZ)]
                moved = [
                    (spectra[q * depth + d, rows, :width], spectra[q * depth + d, rows, width:])
                    for d in range(depth + OUTZ - 1)
                ]
                for w in range(depth):
                    at = (w // 2) * padded + 8 * g
                    shift = (w % 2) * 2 * width
                    a = pattern[at : at + 8, shift : shift + width]
                    b = pattern[at : at + 8, shift + width : shift + 2 * width]
                    for d in range(OUTZ):
                        c, e = moved[w + d]
                        sums[2 * d] = sums[2 * d] + (a * c + b * e)
                        sums[2 * d + 1] = sums[2 * d + 1] + (a * e - b * c)
                for i in range(2 * OUTZ):
                    acc[i, rows, :] = sums[i]
            return carry

        lax.fori_loop(0, edge // depth, body, 0)
        prod = jnp.concatenate(
            [
                jnp.concatenate([acc[2 * d].astype(BF), acc[2 * d + 1].astype(BF)], axis=1)
                for d in range(OUTZ)
            ],
            axis=0,
        )
        back = dot(prod, back_x[...]).astype(BF)
        right = jnp.concatenate(
            [
                jnp.concatenate(
                    [back[d * padded : (d + 1) * padded, i * width : (i + 1) * width] for d in range(OUTZ)],
                    axis=1,
                )
                for i in range(2)
            ],
            axis=0,
        )
        score = dot(back_y[...], right)
        for d in range(OUTZ):
            one = score[:, d * width : (d + 1) * width]
            if begin:
                peak[d] = one
                total[d] = one
            else:
                peak[d] = jnp.maximum(peak[d], one)
                total[d] = total[d] + one

    waiting = sorted(
        ((k, stage) for k in range(chips) for stage in range(bits + 1) if (k, stage) != (0, 0)),
        key=lambda item: (item[0] + item[1], item[0]),
    )

    def serve(level):
        while waiting and sum(waiting[0]) <= level:
            service(*waiting.pop(0))

    fetch.wait()
    pairs = planes // 2
    parts = bits + 1
    for i in range(parts):
        tile_pairs(pairs * i // parts, pairs * (i + 1) // parts)
        serve(i + 1)
    level = parts
    for k in range(chips):
        serve(k + bits)
        rotation(k, 0, k == 0)
        level += 1
        serve(level)
        for h in range(count_t):
            arrive((k, 1, h))
        rotation(k, 1, False)
        level += 1
        serve(level)
    for copy in sends:
        copy.wait_send()


def shards(tiles, live, templates):
    slots, depth, height, width = tiles.shape
    edge = templates.shape[1]
    nb, nt = lax.axis_size("blk"), lax.axis_size("tiles")
    count = templates.shape[0] * nb
    chips = nb // 2
    half = height // 2 + 1
    padded = -(-half // 16) * 16
    groups = -(-half // 8)
    planes = -(-(edge + OUTZ - 1) // 2) * 2
    piece_rows = templates.shape[2] // edge
    own = templates[0].reshape(edge, piece_rows, edge).transpose(1, 0, 2)
    own = own.reshape(piece_rows, edge * edge)
    mats = constants(height, width, edge, padded)
    bits = nt.bit_length() - 1
    n_sends = (chips - 1) + chips * ((nt - 1) + nt)
    vmem = pl.BlockSpec(memory_space=pltpu.VMEM)
    highest, total = pl.pallas_call(
        functools.partial(kernel, (chips, nt, padded, groups, edge, width)),
        out_shape=[jax.ShapeDtypeStruct((OUTZ, height, width), F32)] * 2,
        in_specs=[pl.BlockSpec(memory_space=pl.ANY)] + [vmem] * (1 + len(mats)),
        out_specs=[vmem, vmem],
        scratch_shapes=[
            pltpu.VMEM((planes, height, width), BF),
            pltpu.VMEM((chips, 2, nt, piece_rows, edge * edge), BF),
            pltpu.VMEM((planes, padded, 2 * width), F32),
            pltpu.VMEM((4 * padded, 4 * width), F32),
            pltpu.VMEM((2 * OUTZ, padded, width), F32),
            pltpu.SemaphoreType.DMA,
            pltpu.SemaphoreType.DMA((n_sends,)),
            pltpu.SemaphoreType.DMA((chips, 2, nt)),
        ],
        compiler_params=pltpu.CompilerParams(
            collective_id=0, has_side_effects=True, vmem_limit_bytes=48 * 1024 * 1024
        ),
    )(tiles, own, *mats)
    factor = (live > 0).astype(F32)[:, None, None, None]
    return (highest[None] * factor, total[None] / count * factor)


def solution(mesh):
    placed = (P(("blk", "tiles"), None, None, None), P(("blk", "tiles")), P("blk", None, "tiles"))
    return jax.shard_map(
        shards,
        mesh=mesh,
        in_specs=placed,
        out_specs=(P(("blk", "tiles"), None, None, None), P(("blk", "tiles"), None, None, None)),
        check_vma=False,
    )
```

time: 181 us -> 77 us (0.43)
  matrix products: 82.8 us -> 0 us
  Pallas kernels: 0 us -> 65.8 us
  waiting for transfers between devices: 31.5 us -> 0 us
  local copies, waits for them, and re-layouts: 34.6 us -> 8.8 us
  between operations: 14.8 us -> 1.32 us
  blocking collectives: 13.2 us -> 0 us
    dot_general x86 -> x0, matrix products: 82.8 us -> none  [mult(): return jnp.einsum(form, left, right, preferred_element_type=jnp.float32)]
    pallas_call x0 -> x1, Pallas kernels: none -> 65.8 us  [shards(): pl.pallas_call(functools.partial(kernel, (chips, nt, padded, groups, edge...]
    all_gather x1 -> x0, waiting for transfers between devices: 31.5 us -> none  [shards(): piece = lax.all_gather(whole, 'blk', axis=0, tiled=True)]
    while x34 -> x0, local copies, waits for them, and re-layouts: 17 us -> none
    all_gather x1 -> x0, blocking collectives: 13.2 us -> none  [shards(): whole = lax.all_gather(templates, 'tiles', axis=2, tiled=True)]
    squeeze x8 -> x0, local copies, waits for them, and re-layouts: 9 us -> none  [update(): volume = template.reshape(edge, edge, edge)]
    dynamic_slice x8 -> x0, local copies, waits for them, and re-layouts: 8.64 us -> none  [inner(): return update(state, piece[index])]
    unnamed x2 -> x14, local copies, waits for them, and re-layouts: 0.01 us -> 7.34 us
  transfers between devices with their start and end apart: 1 -> 0, of which waited for: 1 -> 0; matrix products, arithmetic and copies ran while one was open for 9% -> 0% of each run, Pallas kernels for 0% -> 0%
where the time goes in v1:
time: 77 us; the launch traced here: 76.6 us
  Pallas kernels  65.8 us (85%)
  local copies, waits for them, and re-layouts  8.8 us (11%)
  between operations  1.32 us (2%)
    pallas_call x1, Pallas kernels, shards(): pl.pallas_call(functools.partial(kernel, (chips, nt, padded, groups, edge...  65.8 us
    unnamed x14, local copies, waits for them, and re-layouts  7.34 us

profile of v1, /device:TPU:0, one launch (start us, length us, event | category | flops | bytes accessed | tf_op | source)
XLA Modules:
  0.0 76.6 jit_solution(15183400139166950510)
XLA Ops:
  1.3 1.1 %reshape_squeeze.3 = bf16[64,16,64]{2,1,0:T(8,128)(2,1)S(1)} reshape(bf16[1,64,1024]{2,1,0:T(8,128)(2,1)} %param.11) | data formatting | bytes 262144 | tf_op jit(solution)/shard_map/reshape;squeeze | solution.py:263
  2.4 0.1 copy.13
  2.5 0.3 reshape.13.own
  2.8 0.0 copy-start
  2.8 2.2 %copy-done = bf16[1,128,128,128]{3,2,1,0:T(8,128)(2,1)S(1)} copy-done((bf16[1,128,128,128]{3,2,1,0:T(8,128)(2,1)S(1)}, bf16[1,128,128,128]{3,2,1,0:T(8,128)(2,1)}, u32[]{:S(2)}) %copy-start) | copy-done | bytes 4194328
  4.9 0.0 copy-start.1
  5.0 0.9 %copy-done.1 = bf16[256,512]{1,0:T(8,128)(2,1)S(1)} copy-done((bf16[256,512]{1,0:T(8,128)(2,1)S(1)}, bf16[256,512]{1,0:T(8,128)(2,1)}, u32[]{:S(2)}) %copy-start.1) | copy-done | bytes 262168
  5.9 0.0 copy-start.2
  5.9 0.9 %copy-done.2 = bf16[256,256]{1,0:T(8,128)(2,1)S(1)} copy-done((bf16[256,256]{1,0:T(8,128)(2,1)S(1)}, bf16[256,256]{1,0:T(8,128)(2,1)}, u32[]{:S(2)}) %copy-start.2) | copy-done | bytes 131096
  6.8 0.0 copy-start.3
  6.8 0.9 %copy-done.3 = bf16[256,256]{1,0:T(8,128)(2,1)S(1)} copy-done((bf16[256,256]{1,0:T(8,128)(2,1)S(1)}, bf16[256,256]{1,0:T(8,128)(2,1)}, u32[]{:S(2)}) %copy-start.3) | copy-done | bytes 131096
  7.7 0.0 copy-start.4
  7.7 0.8 %copy-done.4 = bf16[128,160]{1,0:T(8,128)(2,1)S(1)} copy-done((bf16[128,160]{1,0:T(8,128)(2,1)S(1)}, bf16[128,160]{1,0:T(8,128)(2,1)}, u32[]{:S(2)}) %copy-start.4) | copy-done | bytes 40984
  8.5 0.0 copy-start.5
  8.6 0.8 %copy-done.5 = bf16[160,64]{1,0:T(8,128)(2,1)S(1)} copy-done((bf16[160,64]{1,0:T(8,128)(2,1)S(1)}, bf16[160,64]{1,0:T(8,128)(2,1)}, u32[]{:S(2)}) %copy-start.5) | copy-done | bytes 20504
  9.3 0.0 copy-start.6
  9.3 0.8 %copy-done.6 = bf16[160,128]{1,0:T(8,128)(2,1)S(1)} copy-done((bf16[160,128]{1,0:T(8,128)(2,1)S(1)}, bf16[160,128]{1,0:T(8,128)(2,1)}, u32[]{:S(2)}) %copy-start.6) | copy-done | bytes 40984
  10.1 65.8 %shard_map.104 = (f32[2,128,128]{2,1,0:T(8,128)S(1)}, f32[2,128,128]{2,1,0:T(8,128)S(1)}) custom-call(bf16[1,128,128,128]{3,2,1,0:T(8,128)(2,1)S(1)} %copy-done, bf16[16,4096]{1,0:T(8,128)(2,1)S(1)} %reshape.13.own, bf16[160,128]{1,0:T(8,128)(2,1)S(1)} %copy-done.6, bf16[160,64]{1,0:T(8,128)(2,1)S(1)} %copy-done.5, bf16[256,256]{1,0:T(8,128)(2,1)S(1)} %copy-done.3, ...), custom_call_target="tpu_custom_call" | custom-call | tf_op jit(solution)/shard_map/pallas_call | solution.py:269
  75.9 0.7 multiply_bitcast_fusion
Async XLA Ops:
  2.8 2.2 %copy-start = (bf16[1,128,128,128]{3,2,1,0:T(8,128)(2,1)S(1)}, bf16[1,128,128,128]{3,2,1,0:T(8,128)(2,1)}, u32[]{:S(2)}) copy-start(bf16[1,128,128,128]{3,2,1,0:T(8,128)(2,1)} %tile_hbm.1) | copy-start | bytes 12582916
  4.9 0.9 %copy-start.1 = (bf16[256,512]{1,0:T(8,128)(2,1)S(1)}, bf16[256,512]{1,0:T(8,128)(2,1)}, u32[]{:S(2)}) copy-start(bf16[256,512]{1,0:T(8,128)(2,1)} %constant.22.clone.pair_x) | copy-start | bytes 786436
  5.9 0.9 %copy-start.2 = (bf16[256,256]{1,0:T(8,128)(2,1)S(1)}, bf16[256,256]{1,0:T(8,128)(2,1)}, u32[]{:S(2)}) copy-start(bf16[256,256]{1,0:T(8,128)(2,1)} %constant.23.clone.back_x) | copy-start | bytes 393220
  6.8 0.9 %copy-start.3 = (bf16[256,256]{1,0:T(8,128)(2,1)S(1)}, bf16[256,256]{1,0:T(8,128)(2,1)}, u32[]{:S(2)}) copy-start(bf16[256,256]{1,0:T(8,128)(2,1)} %constant.21.clone.tile_x) | copy-start | bytes 393220
  7.7 0.8 %copy-start.4 = (bf16[128,160]{1,0:T(8,128)(2,1)S(1)}, bf16[128,160]{1,0:T(8,128)(2,1)}, u32[]{:S(2)}) copy-start(bf16[128,160]{1,0:T(8,128)(2,1)} %constant.24.clone.back_y) | copy-start | bytes 122884
  8.5 0.8 %copy-start.5 = (bf16[160,64]{1,0:T(8,128)(2,1)S(1)}, bf16[160,64]{1,0:T(8,128)(2,1)}, u32[]{:S(2)}) copy-start(bf16[160,64]{1,0:T(8,128)(2,1)} %constant.20.clone.pat_y) | copy-start | bytes 61444
  9.3 0.8 %copy-start.6 = (bf16[160,128]{1,0:T(8,128)(2,1)S(1)}, bf16[160,128]{1,0:T(8,128)(2,1)}, u32[]{:S(2)}) copy-start(bf16[160,128]{1,0:T(8,128)(2,1)} %constant.19.clone.tile_y) | copy-start | bytes 122884

commit v2 on v1

--- a/solution.py
+++ b/solution.py
@@ -10,6 +10,8 @@
 from jax.sharding import PartitionSpec as P
 
 OUTZ = 2
+DEPTH = 32
+TILE_STEP = 4
 MESH = pl.DeviceIdType.MESH
 BF = jnp.bfloat16
 F32 = jnp.float32
@@ -44,7 +46,14 @@
     back_y[:, :half] = cy[:, :half].astype(jnp.bfloat16).astype(np.float32) * weight
     back_y[:, padded : padded + half] = -sy[:, :half].astype(jnp.bfloat16).astype(np.float32) * weight
     parts = (rows, rows[:, :edge], tile_x, pair_x, back_x, back_y)
-    return tuple(jnp.asarray(np.ascontiguousarray(p).astype(jnp.bfloat16)) for p in parts)
+    places, top = [], 0
+    for part in parts:
+        places.append((top, part.shape[0], part.shape[1]))
+        top += part.shape[0]
+    whole = np.zeros((top, max(part.shape[1] for part in parts)), np.float32)
+    for (start, high, wide), part in zip(places, parts):
+        whole[start : start + high, :wide] = part
+    return jnp.asarray(whole.astype(jnp.bfloat16)), places
 
 
 def dot(left, right):
@@ -52,10 +61,13 @@
 
 
 def kernel(
-    cfg, tile_hbm, own, tile_y, pat_y, tile_x, pair_x, back_x, back_y, peak, total,
-    tile_buf, pieces, spectra, pattern, acc, tile_sem, send_sem, recv_sem,
+    cfg, tile_hbm, mats_hbm, own, peak, total,
+    tile_buf, mats, pieces, spectra, pattern, acc, prods, tile_sem, mats_sem, send_sem, recv_sem,
 ):
-    chips, count_t, padded, groups, edge, width = cfg
+    chips, count_t, padded, groups, edge, width, places = cfg
+    tile_y, pat_y, tile_x, pair_x, back_x, back_y = (
+        mats.at[start : start + high, 0:wide] for start, high, wide in places
+    )
     bits = count_t.bit_length() - 1
     planes = tile_buf.shape[0]
     blk = lax.axis_index("blk")
@@ -63,6 +75,8 @@
     chip, core = blk // 2, blk % 2
     fetch = pltpu.make_async_copy(tile_hbm.at[0, pl.ds(0, planes)], tile_buf, tile_sem)
     fetch.start()
+    fetch_mats = pltpu.make_async_copy(mats_hbm, mats, mats_sem)
+    fetch_mats.start()
 
     def other(bit):
         size = 1 << bit
@@ -117,9 +131,12 @@
         send((0, 0, 0), (k, 0, 0), line[k - 1])
     service(0, 0)
 
-    def tile_pairs(low, high):
-        def body(p, carry):
-            both = jnp.concatenate([tile_buf[2 * p], tile_buf[2 * p + 1]], axis=1)
+    pairs = planes // 2
+
+    def tile_pairs(first_pair, count):
+        for p in range(count):
+            at = first_pair + p
+            both = jnp.concatenate([tile_buf[2 * at], tile_buf[2 * at + 1]], axis=1)
             first = dot(tile_y[...], both).astype(BF)
             left = jnp.concatenate(
                 [
@@ -135,15 +152,23 @@
                 axis=0,
             )
             out = dot(left, tile_x[...])
-            spectra[2 * p] = out[:padded]
-            spectra[2 * p + 1] = out[padded:]
+            spectra[2 * at] = out[:padded]
+            spectra[2 * at + 1] = out[padded:]
+
+    def tile_range(low, high):
+        step = TILE_STEP
+
+        def body(i, carry):
+            tile_pairs(low + i * step, step)
             return carry
 
-        lax.fori_loop(low, high, body, 0)
-
-    def rotation(k, side, begin):
+        lax.fori_loop(0, (high - low) // step, body, 0)
+        if (high - low) % step:
+            tile_pairs(high - (high - low) % step, (high - low) % step)
+
+    def rotation(k, side, between):
         acc[...] = jnp.zeros_like(acc)
-        depth = 8
+        depth = DEPTH
         lanes = depth * edge
 
         def body(q, carry):
@@ -190,61 +215,79 @@
                     acc[i, rows, :] = sums[i]
             return carry
 
-        lax.fori_loop(0, edge // depth, body, 0)
-        prod = jnp.concatenate(
-            [
-                jnp.concatenate([acc[2 * d].astype(BF), acc[2 * d + 1].astype(BF)], axis=1)
-                for d in range(OUTZ)
-            ],
-            axis=0,
-        )
-        back = dot(prod, back_x[...]).astype(BF)
-        right = jnp.concatenate(
-            [
-                jnp.concatenate(
-                    [back[d * padded : (d + 1) * padded, i * width : (i + 1) * width] for d in range(OUTZ)],
-                    axis=1,
+        steps = edge // depth
+        lax.fori_loop(0, steps // 2, body, 0)
+        between()
+        lax.fori_loop(steps // 2, steps, body, 0)
+        base = (2 * k + side) * OUTZ * padded
+        for d in range(OUTZ):
+            for i in range(2):
+                prods[base + d * padded : base + (d + 1) * padded, i * width : (i + 1) * width] = (
+                    acc[2 * d + i].astype(BF)
                 )
-                for i in range(2)
-            ],
-            axis=0,
-        )
-        score = dot(back_y[...], right)
+
+    def finish(group, count, begin):
+        rows = count * OUTZ * padded
+        back = dot(prods[group * rows : (group + 1) * rows], back_x[...]).astype(BF)
+        best, added = [None] * OUTZ, [None] * OUTZ
+        for r in range(count):
+            base = r * OUTZ * padded
+            right = jnp.concatenate(
+                [
+                    jnp.concatenate(
+                        [
+                            back[base + d * padded : base + (d + 1) * padded, i * width : (i + 1) * width]
+                            for d in range(OUTZ)
+                        ],
+                        axis=1,
+                    )
+                    for i in range(2)
+                ],
+                axis=0,
+            )
+            score = dot(back_y[...], right)
+            for d in range(OUTZ):
+                one = score[:, d * width : (d + 1) * width]
+                best[d] = one if r == 0 else jnp.maximum(best[d], one)
+                added[d] = one if r == 0 else added[d] + one
         for d in range(OUTZ):
-            one = score[:, d * width : (d + 1) * width]
             if begin:
-                peak[d] = one
-                total[d] = one
+                peak[d] = best[d]
+                total[d] = added[d]
             else:
-                peak[d] = jnp.maximum(peak[d], one)
-                total[d] = total[d] + one
-
-    waiting = sorted(
-        ((k, stage) for k in range(chips) for stage in range(bits + 1) if (k, stage) != (0, 0)),
-        key=lambda item: (item[0] + item[1], item[0]),
-    )
-
-    def serve(level):
-        while waiting and sum(waiting[0]) <= level:
+                peak[d] = jnp.maximum(peak[d], best[d])
+                total[d] = total[d] + added[d]
+
+    order = [(0, stage) for stage in range(1, bits)] + [(k, 0) for k in range(1, chips)]
+    order += [(k, stage) for stage in range(1, bits) for k in range(1, chips)]
+    order.insert(bits + 1, (0, bits))
+    order += [(k, bits) for k in range(1, chips)]
+    waiting = list(order)
+
+    def serve(steps=1):
+        for _ in range(min(steps, len(waiting))):
             service(*waiting.pop(0))
 
+    def need(item):
+        while item in waiting:
+            serve()
+
+    fetch_mats.wait()
     fetch.wait()
-    pairs = planes // 2
     parts = bits + 1
     for i in range(parts):
-        tile_pairs(pairs * i // parts, pairs * (i + 1) // parts)
-        serve(i + 1)
-    level = parts
+        tile_range(pairs * i // parts, pairs * (i + 1) // parts)
+        serve()
     for k in range(chips):
-        serve(k + bits)
-        rotation(k, 0, k == 0)
-        level += 1
-        serve(level)
+        need((k, bits))
+        rotation(k, 0, serve)
+        serve()
         for h in range(count_t):
             arrive((k, 1, h))
-        rotation(k, 1, False)
-        level += 1
-        serve(level)
+        rotation(k, 1, serve)
+        serve()
+        if k % 2 == 1:
+            finish(k // 2, 4, k == 1)
     for copy in sends:
         copy.wait_send()
 
@@ -262,29 +305,32 @@
     piece_rows = templates.shape[2] // edge
     own = templates[0].reshape(edge, piece_rows, edge).transpose(1, 0, 2)
     own = own.reshape(piece_rows, edge * edge)
-    mats = constants(height, width, edge, padded)
+    mats, places = constants(height, width, edge, padded)
     bits = nt.bit_length() - 1
     n_sends = (chips - 1) + chips * ((nt - 1) + nt)
     vmem = pl.BlockSpec(memory_space=pltpu.VMEM)
     highest, total = pl.pallas_call(
-        functools.partial(kernel, (chips, nt, padded, groups, edge, width)),
+        functools.partial(kernel, (chips, nt, padded, groups, edge, width, places)),
         out_shape=[jax.ShapeDtypeStruct((OUTZ, height, width), F32)] * 2,
-        in_specs=[pl.BlockSpec(memory_space=pl.ANY)] + [vmem] * (1 + len(mats)),
+        in_specs=[pl.BlockSpec(memory_space=pl.ANY)] * 2 + [vmem],
         out_specs=[vmem, vmem],
         scratch_shapes=[
             pltpu.VMEM((planes, height, width), BF),
+            pltpu.VMEM(mats.shape, BF),
             pltpu.VMEM((chips, 2, nt, piece_rows, edge * edge), BF),
             pltpu.VMEM((planes, padded, 2 * width), F32),
-            pltpu.VMEM((4 * padded, 4 * width), F32),
+            pltpu.VMEM((DEPTH // 2 * padded, 4 * width), F32),
             pltpu.VMEM((2 * OUTZ, padded, width), F32),
+            pltpu.VMEM((count * OUTZ * padded, 2 * width), BF),
+            pltpu.SemaphoreType.DMA,
             pltpu.SemaphoreType.DMA,
             pltpu.SemaphoreType.DMA((n_sends,)),
             pltpu.SemaphoreType.DMA((chips, 2, nt)),
         ],
         compiler_params=pltpu.CompilerParams(
-            collective_id=0, has_side_effects=True, vmem_limit_bytes=48 * 1024 * 1024
+            collective_id=0, has_side_effects=True, vmem_limit_bytes=60 * 1024 * 1024
         ),
-    )(tiles, own, *mats)
+    )(tiles, mats, own)
     factor = (live > 0).astype(F32)[:, None, None, None]
     return (highest[None] * factor, total[None] / count * factor)
 

time: 77 us -> 48.7 us (0.63)
  Pallas kernels: 65.8 us -> 43.4 us
  local copies, waits for them, and re-layouts: 8.8 us -> 2.12 us
  other arithmetic: 0.72 us -> 1.69 us
    pallas_call x1, Pallas kernels: 65.8 us -> 43.4 us  [shards(): pl.pallas_call(functools.partial(kernel, (chips, nt, padded, groups, edge...]
    unnamed x14 -> x0, local copies, waits for them, and re-layouts: 7.34 us -> none
    mul x1, other arithmetic: 0.72 us -> 1.69 us  [shards(): return (highest[None] * factor, total[None] / count * factor)]
where the time goes in v2:
time: 48.7 us; the launch traced here: 48.6 us
  Pallas kernels  43.4 us (89%)
  local copies, waits for them, and re-layouts  2.12 us (4%)
  other arithmetic  1.69 us (3%)
  between operations  1.3 us (3%)
    pallas_call x1, Pallas kernels, shards(): pl.pallas_call(functools.partial(kernel, (chips, nt, padded, groups, edge...  43.4 us
    mul x1, other arithmetic, shards(): return (highest[None] * factor, total[None] / count * factor)  1.69 us
    another operation x2, local copies, waits for them, and re-layouts, shards(): own = templates[0].reshape(edge, piece_rows, edge).transpose(1, 0, 2)  1.19 us

profile of v2, /device:TPU:0, one launch (start us, length us, event | category | flops | bytes accessed | tf_op | source)
XLA Modules:
  0.0 48.6 jit_solution(6003035074629708074)
XLA Ops:
  1.3 1.1 %reshape_squeeze.3 = bf16[64,16,64]{2,1,0:T(8,128)(2,1)S(1)} reshape(bf16[1,64,1024]{2,1,0:T(8,128)(2,1)} %param.6) | data formatting | bytes 262144 | tf_op jit(solution)/shard_map/reshape;squeeze | solution.py:306
  2.4 0.1 copy.8
  2.5 0.9 %reshape.13.own = bf16[16,4096]{1,0:T(8,128)(2,1)} reshape(bf16[16,64,64]{2,1,0:T(8,128)(2,1)S(1)} %bitcast.9) | data formatting | bytes 262144 | tf_op jit(solution)/shard_map/reshape | solution.py:307
  3.4 43.4 %shard_map.59 = (f32[2,128,128]{2,1,0:T(8,128)}, f32[2,128,128]{2,1,0:T(8,128)}) custom-call(bf16[1,128,128,128]{3,2,1,0:T(8,128)(2,1)} %tile_hbm.1, bf16[1216,512]{1,0:T(8,128)(2,1)} %constant.9.clone.mats_hbm, bf16[16,4096]{1,0:T(8,128)(2,1)} %reshape.13.own), custom_call_target="tpu_custom_call" | custom-call | tf_op jit(solution)/shard_map/pallas_call | solution.py:312
  46.9 1.7 %multiply_bitcast_fusion = (f32[1,2,128,128]{3,2,1,0:T(8,128)}, f32[1,2,128,128]{3,2,1,0:T(8,128)}) fusion(f32[2,128,128]{2,1,0:T(8,128)} %get-tuple-element.5, f32[]{:T(128)} %bitcast.3, f32[2,128,128]{2,1,0:T(8,128)} %get-tuple-element.4, f32[]{:T(128)} %bitcast.1), kind=kLoop, calls=%fused_computation.1 | loop fusion | flops 65536 | bytes 524296 | tf_op jit(solution)/shard_map/mul | solution.py:335
